TPU v7x, 32 devices: a whole 2x2x4 slice. The times are simulated.
32 devices in a mesh: space: 16 (over z, y, x), feat: 2 (over core).
Axes of the slice: x: 2, y: 2, z: 4, core: 2. Of those that a mesh axis runs over, the one named last changes fastest.
Arguments:
- nodes: bfloat16 [2560, 512], P('space'), may hold values from -6 to 6
- edges: bfloat16 [12288, 512], P(('space', 'feat')), may hold values from -6 to 6
- senders: int32 [12288], P(('space', 'feat')), may hold values from 0 to 2559, as said below
- receivers: int32 [12288], P(('space', 'feat')), may hold values from 0 to 2559, as said below
- edge_proj: bfloat16 [512, 512], replicated, may hold values from -0.15625 to 0.15625
- send_proj: bfloat16 [512, 512], replicated, may hold values from -0.15625 to 0.15625
- recv_proj: bfloat16 [512, 512], replicated, may hold values from -0.15625 to 0.15625
- edge_bias: float32 [512], replicated, may hold values from -3 to 3
- edge_out: bfloat16 [512, 512], replicated, may hold values from -0.25 to 0.25
- edge_gain: float32 [512], replicated, may hold values from 0.25 to 1.75
- edge_shift: float32 [512], replicated, may hold values from -3 to 3
- node_in: bfloat16 [1024, 512], replicated, may hold values from -0.1875 to 0.1875
- node_bias: float32 [512], replicated, may hold values from -3 to 3
- node_out: bfloat16 [512, 512], replicated, may hold values from -0.25 to 0.25
- node_gain: float32 [512], replicated, may hold values from 0.25 to 1.75
- node_shift: float32 [512], replicated, may hold values from -3 to 3
- node_cot: bfloat16 [2560, 512], P('space'), may hold values from -6 to 6
Outputs:
- new_nodes: bfloat16 [2560, 512], P('space')
- node_grad: bfloat16 [2560, 512], P('space')
- edge_grad: bfloat16 [12288, 512], P(('space', 'feat'))
Inputs may be any that keep to these rules, and one draw needn't show every extreme that they name: `senders`: every edge of a block's 768 has its receiver in that block; its sender lies in the same block, in the last 48 rows of the previous block, in the first 48 rows of the next block, or among the first 2 rows of any block. `receivers`: every edge of a block's 768 has its receiver among that block's 160 nodes.
All inputs are finite; a program needn't handle non-finite values.
Results may differ from a plain program's by a relative error of at most 0.0077.
Values may be sent and summed in bfloat16 or wider, within the bound.
A program may use at most 64 MiB of HBM per device.

v0:
```python
import jax
import jax.numpy as jnp
from jax import lax
from jax.sharding import PartitionSpec as P

RIM = 48
HUB_DEV = 2


epsilon = 1e-05


def padded(block, sides, width):
    for axis, dim in sides:
        count = lax.axis_size(axis)
        forward = [(i, i + 1) for i in range(count - 1)]
        backward = [(target, source) for source, target in forward]
        low = lax.ppermute(
            lax.slice_in_dim(block, block.shape[dim] - width, None, axis=dim), axis, forward
        )
        high = lax.ppermute(lax.slice_in_dim(block, 0, width, axis=dim), axis, backward)
        block = jnp.concatenate([low, block, high], axis=dim)
    return block


def layer_stats(values):
    average = jnp.mean(values, axis=-1, keepdims=True)
    centred = values - average
    inv_scale = lax.rsqrt(jnp.mean(centred * centred, axis=-1, keepdims=True) + epsilon)
    return (centred * inv_scale, inv_scale)


def norm_back(upstream, normed, inv_scale, gain_vec):
    scaled = upstream * gain_vec
    return inv_scale * (
        scaled
        - jnp.mean(scaled, axis=-1, keepdims=True)
        - normed * jnp.mean(scaled * normed, axis=-1, keepdims=True)
    )


def swish_slope(preact):
    sigmoid_val = jax.nn.sigmoid(preact)
    return sigmoid_val * (1.0 + preact * (1.0 - sigmoid_val))


def feat_total(partial_sum):
    return lax.psum(partial_sum, "feat")


def column_sums(onehot, values):
    return lax.dot_general(
        onehot, values, (((0,), (0,)), ((), ())), preferred_element_type=jnp.float32
    )


def exact_dot(left, right):
    return jnp.dot(left, right, precision=lax.Precision.HIGHEST)


def body(
    nodes,
    edges,
    senders,
    receivers,
    edge_proj,
    send_proj,
    recv_proj,
    edge_bias,
    edge_out,
    edge_gain,
    edge_shift,
    node_in,
    node_bias,
    node_out,
    node_gain,
    node_shift,
    node_cot,
):
    node_count = nodes.shape[0]
    width = nodes.shape[1]
    feat_count = lax.axis_size("feat")
    feat_index = lax.axis_index("feat")
    own_block = lax.axis_index("space")
    hub_total = HUB_DEV * lax.axis_size("space")
    table_count = 2 * RIM + node_count + hub_total
    edge_rows = lax.all_gather(edges, "feat", axis=0, tiled=True)
    send_ids, recv_ids = (
        lax.all_gather(senders, "feat", axis=0, tiled=True),
        lax.all_gather(receivers, "feat", axis=0, tiled=True),
    )
    half_width = width // feat_count
    col_start = feat_index * half_width
    w_edge = lax.dynamic_slice_in_dim(edge_proj, col_start, half_width, 1)
    w_send = lax.dynamic_slice_in_dim(send_proj, col_start, half_width, 1)
    w_recv = lax.dynamic_slice_in_dim(recv_proj, col_start, half_width, 1)
    bias_part = lax.dynamic_slice_in_dim(edge_bias, col_start, half_width, 0)
    w_out = lax.dynamic_slice_in_dim(edge_out, col_start, half_width, 0)
    edge_count = edge_rows.shape[0]
    col_count = w_send.shape[1]
    sender_block = send_ids // node_count
    sender_row = send_ids - sender_block * node_count
    from_own = sender_block == own_block
    from_left = (sender_block == own_block - 1) & (sender_row >= node_count - RIM)
    from_right = (sender_block == own_block + 1) & (sender_row < RIM)
    slot_index = jnp.where(
        from_own,
        RIM + sender_row,
        jnp.where(
            from_left,
            sender_row - (node_count - RIM),
            jnp.where(
                from_right,
                RIM + node_count + sender_row,
                2 * RIM + node_count + sender_block * HUB_DEV + sender_row,
            ),
        ),
    )
    local_recv = recv_ids - own_block * node_count
    slot_onehot = (slot_index[:, None] == jnp.arange(table_count, dtype=jnp.int32)[None, :]).astype(
        jnp.bfloat16
    )
    recv_onehot = (local_recv[:, None] == jnp.arange(node_count, dtype=jnp.int32)[None, :]).astype(
        jnp.bfloat16
    )
    carried = jnp.dot(nodes, send_proj, preferred_element_type=jnp.float32).astype(jnp.bfloat16)
    framed = padded(carried, (("space", 0),), RIM)
    coarse = lax.all_gather(carried[:HUB_DEV], "space", axis=0, tiled=True)
    table_rows = jnp.concatenate([framed, coarse], axis=0)
    send_terms = lax.dynamic_slice_in_dim(table_rows, col_start, col_count, 1)
    recv_terms = jnp.dot(nodes, w_recv, preferred_element_type=jnp.float32).astype(jnp.bfloat16)
    hidden_pre = (
        jnp.dot(edge_rows, w_edge, preferred_element_type=jnp.float32)
        + jnp.dot(slot_onehot, send_terms, preferred_element_type=jnp.float32)
        + jnp.dot(recv_onehot, recv_terms, preferred_element_type=jnp.float32)
        + bias_part
    )
    hidden_act = jax.nn.silu(hidden_pre).astype(jnp.bfloat16)
    edge_sum = jnp.dot(hidden_act, w_out, preferred_element_type=jnp.float32)
    edge_sum = feat_total(edge_sum)
    edge_normed, edge_scale = layer_stats(edge_sum)
    new_edges = (edge_rows.astype(jnp.float32) + edge_normed * edge_gain + edge_shift).astype(
        jnp.bfloat16
    )
    gathered_wide = column_sums(recv_onehot, new_edges)
    gathered = gathered_wide.astype(jnp.bfloat16)
    node_pre = (
        jnp.dot(nodes, node_in[:width], preferred_element_type=jnp.float32)
        + jnp.dot(gathered, node_in[width:], preferred_element_type=jnp.float32)
        + node_bias
    )
    node_act = jax.nn.silu(node_pre).astype(jnp.bfloat16)
    node_mix = jnp.dot(node_act, node_out, preferred_element_type=jnp.float32)
    node_normed, node_scale = layer_stats(node_mix)
    new_nodes = (nodes.astype(jnp.float32) + node_normed * node_gain + node_shift).astype(
        jnp.bfloat16
    )
    upstream = node_cot.astype(jnp.float32)
    node_dmix = norm_back(upstream, node_normed, node_scale, node_gain).astype(jnp.bfloat16)
    node_dact = jnp.dot(node_dmix, node_out.T, preferred_element_type=jnp.float32)
    node_dpre = (node_dact * swish_slope(node_pre)).astype(jnp.bfloat16)
    node_direct = upstream + jnp.dot(
        node_dpre, node_in[:width].T, preferred_element_type=jnp.float32
    )
    gathered_grad = jnp.dot(node_dpre, node_in[width:].T, preferred_element_type=jnp.float32)
    edge_upstream = exact_dot(recv_onehot.astype(jnp.float32), gathered_grad)
    edge_dsum = norm_back(edge_upstream, edge_normed, edge_scale, edge_gain).astype(jnp.bfloat16)
    edge_dact = jnp.dot(edge_dsum, w_out.T, preferred_element_type=jnp.float32)
    edge_dpre = (edge_dact * swish_slope(hidden_pre)).astype(jnp.bfloat16)
    edge_part = jnp.dot(edge_dpre, w_edge.T, preferred_element_type=jnp.float32)
    recv_sums = column_sums(recv_onehot, edge_dpre)
    slot_sums = column_sums(slot_onehot, edge_dpre)
    recv_part = exact_dot(recv_sums, w_recv.astype(jnp.float32).T)
    rim_terms = jnp.concatenate(
        [slot_sums[:RIM], slot_sums[RIM + node_count : 2 * RIM + node_count]], axis=0
    )
    rim_back = padded(rim_terms.astype(jnp.bfloat16), (("space", 0),), RIM).astype(rim_terms.dtype)
    hub_back = lax.psum_scatter(
        slot_sums[2 * RIM + node_count :], "space", scatter_dimension=0, tiled=True
    )
    own_terms = slot_sums[RIM : RIM + node_count]
    own_terms = own_terms + jnp.pad(rim_back[:RIM], ((0, node_count - RIM), (0, 0)))
    own_terms = own_terms + jnp.pad(rim_back[3 * RIM :], ((node_count - RIM, 0), (0, 0)))
    own_terms = own_terms + jnp.pad(hub_back, ((0, node_count - HUB_DEV), (0, 0)))
    own_terms = exact_dot(own_terms, w_send.astype(jnp.float32).T)
    totals = feat_total(jnp.concatenate([edge_part, own_terms + recv_part], axis=0))
    edge_full = edge_upstream + totals[:edge_count]
    node_extra = totals[edge_count:]
    own_edges = edge_count // feat_count
    edge_grad = lax.dynamic_slice_in_dim(edge_full, feat_index * own_edges, own_edges, 0).astype(
        jnp.bfloat16
    )
    node_grad = (node_direct + node_extra).astype(jnp.bfloat16)
    return (new_nodes, node_grad, edge_grad)


def solution(mesh):
    in_specs = (
        P("space", None),
        P(("space", "feat"), None),
        P(("space", "feat")),
        P(("space", "feat")),
        P(),
        P(),
        P(),
        P(),
        P(),
        P(),
        P(),
        P(),
        P(),
        P(),
        P(),
        P(),
        P("space", None),
    )
    out_specs = (P("space", None), P("space", None), P(("space", "feat"), None))
    return jax.shard_map(body, mesh=mesh, in_specs=in_specs, out_specs=out_specs, check_vma=False)
```

profile of v0, /device:TPU:0, one launch (start us, length us, event | category | flops | bytes accessed | tf_op | source)
XLA Modules:
  0.0 216.2 jit_solution(7370596817582496482)
XLA Ops:
  7.2 0.0 copy-start
  7.2 0.0 copy-start.11
  7.2 0.0 all-reduce.6.cloned.1.call-start
  7.2 1.5 convolution_convert_fusion.1
  8.7 0.0 copy-start.18
  8.7 1.3 collective-permute-start.1
  10.0 5.5 %collective-permute-start = (bf16[48,512]{1,0:T(8,128)(2,1)S(1)}, bf16[48,512]{1,0:T(8,128)(2,1)S(1)}, u32[]{:S(2)}, u32[]{:S(2)}) collective-permute-start(bf16[48,512]{1,0:T(8,128)(2,1)S(1)} %get-tuple-element.9), channel_id=1, source_target_pairs={{0,2},{2,4},{4,6},{6,8},{8,10},{10,12},{12,14},{14,16},{16,18},{18... | collective-permute-start | bytes 147464 | tf_op jit(solution)/shard_map/ppermute | solution.py:18
  15.5 0.7 reshape.56
  16.2 1.8 all-gather.1
  18.0 0.7 reshape.54
  18.7 1.8 all-gather
  20.5 2.6 %all_gather.13 = bf16[768,512]{1,0:T(8,128)(2,1)S(1)} all-gather(bf16[384,512]{1,0:T(8,128)(2,1)} %param.18), channel_id=1, replica_groups=mesh['space'=16,'feat'=2] {'feat'}, dimensions={0}, use_global_device_ids=true | all-gather | bytes 1179648 | tf_op jit(solution)/shard_map/all_gather | solution.py:87
  23.1 0.0 copy-start.5
  23.1 0.4 convolution_bitcast_fusion
  23.6 0.1 dynamic_slice.24
  23.6 39.5 %all-gather.2 = bf16[16,2,512]{2,1,0:T(2,128)(2,1)S(1)} all-gather(bf16[1,2,512]{2,1,0:T(2,128)(2,1)S(1)} %slice_bitcast_fusion), channel_id=1, replica_groups=mesh['space'=16,'feat'=2] {'space'}, dimensions={0}, use_global_device_ids=true | all-gather | bytes 34816 | tf_op jit(solution)/shard_map/all_gather | solution.py:128
  63.2 0.0 collective-permute-done.1
  63.2 0.0 collective-permute-done
  63.2 0.6 convolution_add_fusion.1
  63.7 1.5 fusion
  65.3 0.9 copy-done.8
  66.2 1.6 fusion.34
  67.7 0.0 all-reduce.6.cloned.1.call-update
  67.8 0.0 all-reduce.8.cloned.1.call-start
  67.8 0.6 copy-done.22
  68.4 0.6 dynamic-slice
  69.6 0.2 fusion.29
  69.9 0.0 copy-start.17
  69.9 0.0 copy-start.20
  69.9 0.0 copy-start.21
  69.9 14.2 %all-reduce.6.cloned.1.call-done = f32[768,512]{1,0:T(8,128)} async-done(((f32[768,512]{1,0:T(8,128)}), f32[768,512]{1,0:T(8,128)}) %all-reduce.6.cloned.1.call-update) | async-done | bytes 1572880 | tf_op jit(solution)/shard_map/psum | solution.py:48
  84.2 1.7 reduce_sum.72
  85.9 0.2 copy-done.1
  86.1 0.3 multiply_reduce_fusion.1
  86.4 2.7 %fusion.2 = f32[160,512]{1,0:T(8,128)} fusion(f32[160,512]{1,0:T(8,128)S(1)} %fusion.29, bf16[768,512]{1,0:T(8,128)(2,1)S(1)} %all_gather.13, f32[768,512]{1,0:T(8,128)S(1)} %copy-done.1, f32[512]{0:T(512)S(1)} %copy-done.20, f32[512]{0:T(512)S(1)} %copy-done.17, f32[768]{0:T(1024)S(1)} %add_rsqrt_fusion, f32[768]{0:T(1024)S(1)} %broadcast_multiply_fusion.2, ...), kind=kOutput, calls=%fused_computation.17 | convolution fusion | flops 212836352 | bytes 3554304 | tf_op jit(solution)/shard_map/dot_general | solution.py:149
  89.2 0.0 copy-start.23
  89.2 1.6 fusion.94
  90.8 0.2 multiply_reduce_fusion.3
  91.0 0.8 fusion.33
  91.9 0.4 fusion.5
  92.2 0.8 copy-done.7
  93.1 0.3 fusion.25
  93.4 1.2 multiply_reduce_fusion.2
  94.7 1.3 fusion.1
  96.0 0.0 copy-start.12
  96.0 1.2 fusion.35
  97.2 0.5 fusion.95
  97.7 0.0 copy-start.14
  97.7 0.4 fusion.54
  98.2 0.3 copy-done.14
  98.4 77.6 %all-reduce.2 = f32[32,256]{1,0:T(8,128)} all-reduce(f32[32,256]{1,0:T(8,128)S(1)} %slice.66), channel_id=2, replica_groups=mesh['space'=16,'feat'=2] {'space'}, use_global_device_ids=true, to_apply=%region_9.10.clone | all-reduce | flops 8192 | bytes 65536
  176.0 1.4 collective-permute-start.2
  177.4 1.3 collective-permute-start.3
  178.7 0.7 constant_dynamic-slice_fusion
  179.4 3.7 %collective-permute-done.3 = bf16[48,256]{1,0:T(8,128)(2,1)S(1)} collective-permute-done((bf16[48,256]{1,0:T(8,128)(2,1)S(1)}, bf16[48,256]{1,0:T(8,128)(2,1)S(1)}, u32[]{:S(2)}, u32[]{:S(2)}) %collective-permute-start.3) | collective-permute-done | bytes 24608 | tf_op jit(solution)/shard_map/ppermute | solution.py:21
  183.2 1.5 fusion.47
  184.7 1.3 convolution_add_fusion.2
  186.0 1.4 pad_maximum_fusion
  187.5 0.0 all-reduce.8.cloned.1.call-update
  187.5 17.8 %all-reduce.8.cloned.1.call-done = f32[928,512]{1,0:T(8,128)} async-done(((f32[928,512]{1,0:T(8,128)}), f32[928,512]{1,0:T(8,128)}) %all-reduce.8.cloned.1.call-update) | async-done | bytes 1900560 | tf_op jit(solution)/shard_map/psum | solution.py:48
  205.3 1.4 slice-done
  206.7 0.9 fusion.7
  207.5 0.8 copy-done.4
  208.3 1.0 fusion.6
  (53 shorter events, 0.2 us)
Async XLA Ops:
  7.2 59.0 %copy-start = (bf16[512,512]{1,0:T(8,128)(2,1)S(1)}, bf16[512,512]{1,0:T(8,128)(2,1)}, u32[]{:S(2)}) copy-start(bf16[512,512]{1,0:T(8,128)(2,1)} %param.25) | copy-start | bytes 1572868
  7.2 15.9 %copy-start.11 = (bf16[512,512]{1,0:T(8,128)(2,1)S(1)}, bf16[512,512]{1,0:T(8,128)(2,1)}, u32[]{:S(2)}) copy-start(bf16[512,512]{1,0:T(8,128)(2,1)} %param.21) | copy-start | bytes 1572868
  7.2 77.0 %all-reduce.6.cloned.1.call-start = ((), (), s32[]{:S(2)}) async-start(), calls=%async_computation | async-start | bytes 3145728 | tf_op jit(solution)/shard_map/psum | solution.py:48
  8.7 14.8 %copy-start.18 = (f32[512]{0:T(512)S(1)}, f32[512]{0:T(512)}, u32[]{:S(2)}) copy-start(f32[512]{0:T(512)} %param.24) | copy-start | bytes 6148
  8.7 54.4 %collective-permute-start.1 = (bf16[48,512]{1,0:T(8,128)(2,1)S(1)}, bf16[48,512]{1,0:T(8,128)(2,1)S(1)}, u32[]{:S(2)}, u32[]{:S(2)}) collective-permute-start(bf16[48,512]{1,0:T(8,128)(2,1)S(1)} %get-tuple-element.8), channel_id=1, source_target_pairs={{2,0},{4,2},{6,4},{8,6},{10,8},{12,10},{14,12},{16,14},{18,16},{20... | collective-permute-start | bytes 147464 | tf_op jit(solution)/shard_map/ppermute | solution.py:21
  10.0 53.1 %collective-permute-start = (bf16[48,512]{1,0:T(8,128)(2,1)S(1)}, bf16[48,512]{1,0:T(8,128)(2,1)S(1)}, u32[]{:S(2)}, u32[]{:S(2)}) collective-permute-start(bf16[48,512]{1,0:T(8,128)(2,1)S(1)} %get-tuple-element.9), channel_id=1, source_target_pairs={{0,2},{2,4},{4,6},{6,8},{8,10},{10,12},{12,14},{14,16},{16,18},{18... | collective-permute-start | bytes 147464 | tf_op jit(solution)/shard_map/ppermute | solution.py:18
  23.1 40.7 %copy-start.5 = (bf16[160,512]{1,0:T(8,128)(2,1)S(1)}, bf16[160,512]{1,0:T(8,128)(2,1)}, u32[]{:S(2)}) copy-start(bf16[160,512]{1,0:T(8,128)(2,1)} %param.17) | copy-start | bytes 491524
  65.2 0.9 copy-start.8
  67.7 0.7 copy-start.22
  67.7 1.9 copy-start.6
  67.8 137.5 %all-reduce.8.cloned.1.call-start = ((), (), s32[]{:S(2)}) async-start(), calls=%async_computation.1 | async-start | bytes 3801088 | tf_op jit(solution)/shard_map/psum | solution.py:48
  69.9 16.5 %copy-start.17 = (f32[512]{0:T(512)S(1)}, f32[512]{0:T(512)}, u32[]{:S(2)}) copy-start(f32[512]{0:T(512)} %param.26) | copy-start | bytes 6148
  69.9 16.5 %copy-start.20 = (f32[512]{0:T(512)S(1)}, f32[512]{0:T(512)}, u32[]{:S(2)}) copy-start(f32[512]{0:T(512)} %param.27) | copy-start | bytes 6148
  69.9 16.5 %copy-start.21 = (f32[512]{0:T(512)S(1)}, f32[512]{0:T(512)}, u32[]{:S(2)}) copy-start(f32[512]{0:T(512)} %param.29) | copy-start | bytes 6148
  84.2 1.9 copy-start.1
  89.1 1.8 copy-start.10
  89.1 1.8 copy-start.15
  89.1 1.9 copy-start.16
  89.1 2.7 %copy-start.19 = (bf16[512,512]{1,0:T(8,128)(2,1)S(1)}, bf16[512,512]{1,0:T(8,128)(2,1)}, u32[]{:S(2)}) copy-start(bf16[512,512]{1,0:T(8,128)(2,1)} %param.30) | copy-start | bytes 1572868
  89.2 2.7 %copy-start.23 = (f32[160,512]{1,0:T(8,128)S(1)}, f32[160,512]{1,0:T(8,128)}, u32[]{:S(2)}) copy-start(f32[160,512]{1,0:T(8,128)} %fusion.2) | copy-start | bytes 983044
  91.8 1.2 copy-start.7
  93.4 1.3 copy-start.9
  94.6 1.3 copy-start.2
  96.0 1.7 copy-start.12
  97.7 0.7 copy-start.14
  176.0 8.7 %copy-start.13 = (bf16[512,512]{1,0:T(8,128)(2,1)S(1)}, bf16[512,512]{1,0:T(8,128)(2,1)}, u32[]{:S(2)}) copy-start(bf16[512,512]{1,0:T(8,128)(2,1)} %param.23) | copy-start | bytes 1572868
  176.0 3.4 %collective-permute-start.2 = (bf16[48,256]{1,0:T(8,128)(2,1)S(1)}, bf16[48,256]{1,0:T(8,128)(2,1)S(1)}, u32[]{:S(2)}, u32[]{:S(2)}) collective-permute-start(bf16[48,256]{1,0:T(8,128)(2,1)S(1)} %get-tuple-element.10), channel_id=1, source_target_pairs={{0,2},{2,4},{4,6},{6,8},{8,10},{10,12},{12,14},{14,16},{16,18},{18... | collective-permute-start | bytes 73736 | tf_op jit(solution)/shard_map/ppermute | solution.py:18
  177.4 5.7 %collective-permute-start.3 = (bf16[48,256]{1,0:T(8,128)(2,1)S(1)}, bf16[48,256]{1,0:T(8,128)(2,1)S(1)}, u32[]{:S(2)}, u32[]{:S(2)}) collective-permute-start(bf16[48,256]{1,0:T(8,128)(2,1)S(1)} %get-tuple-element.11), channel_id=1, source_target_pairs={{2,0},{4,2},{6,4},{8,6},{10,8},{12,10},{14,12},{16,14},{18,16},{20... | collective-permute-start | bytes 73736 | tf_op jit(solution)/shard_map/ppermute | solution.py:21
  187.5 17.8 %copy-start.3 = (f32[768,512]{1,0:T(8,128)S(1)}, f32[768,512]{1,0:T(8,128)}, u32[]{:S(2)}) copy-start(f32[768,512]{1,0:T(8,128)} %copy-done.2) | copy-start | bytes 4718596
  205.3 1.4 slice-start
  206.7 1.7 copy-start.4
Sparse Core Ops, SparseCore 0:
  67.9 16.2 all-reduce.5
  187.6 17.6 all-reduce.7
where the time goes:
time: 217 us; the launch traced here: 216 us
  blocking collectives  123 us (57%)
  waiting for transfers between devices  35.8 us (16%)
  matrix products  19.2 us (9%)
  between operations  15.2 us (7%)
  starting transfers between devices  9.55 us (4%)
  local copies, waits for them, and re-layouts  7.86 us (4%)
  other arithmetic  5.47 us (3%)
    unnamed x1, blocking collectives  77.6 us
    all_gather x1, blocking collectives, body(): coarse = lax.all_gather(carried[:HUB_DEV], 'space', axis=0, tiled=True)  39.5 us
    psum x2, waiting for transfers between devices, feat_total(): return lax.psum(partial_sum, 'feat')  32 us
    ppermute x2, starting transfers between devices, padded(): lax.ppermute(lax.slice_in_dim(block, block.shape[dim] - width, None, axis...  6.88 us
    unnamed x55, local copies, waits for them, and re-layouts  6.35 us
  transfers between devices with their start and end apart: 6, of which 3 were waited for; matrix products, arithmetic and copies ran while one was open for 2% of the time, Pallas kernels for 0%

commit v1 on v0

v1 whole, which is shorter than its diff:
```python
import functools

import jax
import jax.numpy as jnp
from jax import lax
from jax.experimental import pallas as pl
from jax.experimental.pallas import tpu as pltpu
from jax.sharding import PartitionSpec as P

RIM = 48
HUB_DEV = 2
LANES = 128
CHUNK = 64
epsilon = 1e-05

F32 = jnp.float32
BF16 = jnp.bfloat16
MESH = pl.DeviceIdType.MESH


def mm(a, b):
    return jnp.dot(a, b, preferred_element_type=F32)


def mm_t(a, b):
    return lax.dot_general(a, b, (((1,), (1,)), ((), ())), preferred_element_type=F32)


def sigmoid(v):
    return 0.5 * jnp.tanh(0.5 * v) + 0.5


def mean_row(v):
    return jnp.mean(v, axis=-1, keepdims=True)


def late_ids(index, own_block, blocks, rows):
    left = (own_block * rows - RIM) + index
    right = (own_block + 1) * rows + (index - RIM)
    hub = index - 2 * RIM
    row = jnp.zeros_like(hub)
    for step in range(1, HUB_DEV):
        row = row + jnp.where(hub >= step * blocks, 1, 0)
    block = hub - row * blocks
    hub_id = block * rows + row
    hub_id = jnp.where((block == own_block) | (block == own_block + 1), -1, hub_id)
    return jnp.where(index < RIM, left, jnp.where(index < 2 * RIM, right, hub_id))


def onehot(a, b):
    return jnp.where(a == b, 1.0, 0.0).astype(BF16)


def kernel(
    blocks,
    send_id, recv_id, nodes, edges, w_edge, w_send, w_recv, bias, w_out, gain_e, shift_e,
    w_in, bias_n, w_mix, gain_n, shift_n, cot,
    out_nodes, out_grad, out_edges,
    v_send_id, v_recv_id, v_nodes, v_edges, v_edge, v_send, v_recv, v_bias, v_out, v_gain_e, v_shift_e,
    v_in, v_bias_n, v_mix, v_gain_n, v_shift_n, v_cot,
    v_late, v_hub_src, v_hub, oh_own, oh_recv, oh_late,
    v_hidden, v_slope, v_act, v_normed, v_scale, v_new,
    g_mine, g_peer, v_pre, v_dpre, v_direct, v_up, v_dsum, v_edpre,
    rim_out, rim_back, hub_out, hub_back, p_mine, p_peer, x_mine, x_peer,
    o_nodes, o_grad, o_edges,
    load_sem, store_sem, rim_send, rim_recv, hub_send, hub_recv, peer_send, peer_recv,
):
    me = lax.axis_index("space")
    core = lax.axis_index("feat")
    rows, width = v_nodes.shape
    count = v_edges.shape[0]
    pieces = width // LANES
    tile = HUB_DEV * pieces
    peer = (me, 1 - core)
    left, right = (me - 1, core), (me + 1, core)
    has_left, has_right = me > 0, me < blocks - 1

    barrier = pltpu.get_barrier_semaphore()

    def greet(step, carry):
        other = lax.rem(me + step, blocks)
        pl.semaphore_signal(barrier, inc=1, device_id=(other, core), device_id_type=MESH)
        return carry

    lax.fori_loop(1, blocks, greet, 0)
    pl.semaphore_signal(barrier, inc=1, device_id=peer, device_id_type=MESH)

    pairs = [
        (nodes, v_nodes), (send_id, v_send_id), (recv_id, v_recv_id), (w_recv, v_recv), (w_send, v_send),
        (edges, v_edges), (w_edge, v_edge), (bias, v_bias), (w_out, v_out), (gain_e, v_gain_e), (shift_e, v_shift_e),
        (w_in, v_in), (bias_n, v_bias_n), (w_mix, v_mix), (gain_n, v_gain_n), (shift_n, v_shift_n), (cot, v_cot),
    ]
    loads = [pltpu.make_async_copy(src, dst, load_sem.at[k]) for k, (src, dst) in enumerate(pairs)]
    for load in loads:
        load.start()

    def ready(*refs):
        for k, (_, dst) in enumerate(pairs):
            if any(dst is ref for ref in refs):
                loads[k].wait()

    def remote(src, dst, send_sem, recv_sem, device):
        return pltpu.make_async_remote_copy(
            src_ref=src, dst_ref=dst, send_sem=send_sem, recv_sem=recv_sem, device_id=device, device_id_type=MESH
        )

    my_slot = pl.ds(pl.multiple_of(me * tile, tile), tile)

    def hub_copy(step, src, dst, kind):
        other = lax.rem(me + step, blocks)
        return remote(src(other), dst.at[my_slot], hub_send.at[kind], hub_recv.at[kind], (other, core))

    def hub_wait(buffer, sem):
        part = buffer.at[pl.ds(0, (blocks - 1) * tile)]
        pltpu.make_async_copy(part, part, sem).wait()

    ready(v_nodes)
    head = v_nodes[0:16, :].astype(F32)
    for j in range(pieces):
        v_hub_src[HUB_DEV * j : HUB_DEV * (j + 1), :] = head[0:HUB_DEV, LANES * j : LANES * (j + 1)]
    v_hub[my_slot, :] = v_hub_src[...]
    hub_back[my_slot, :] = jnp.zeros((tile, LANES), F32)
    zero_rim = jnp.zeros((RIM, width), BF16)

    @pl.when(jnp.logical_not(has_left))
    def _():
        v_late[0:RIM, :] = zero_rim
        rim_back[0:RIM, :] = zero_rim

    @pl.when(jnp.logical_not(has_right))
    def _():
        v_late[RIM : 2 * RIM, :] = zero_rim
        rim_back[RIM : 2 * RIM, :] = zero_rim

    pl.semaphore_wait(barrier, blocks)

    low, high = pl.ds(0, RIM), pl.ds(RIM, RIM)
    to_right = remote(nodes.at[pl.ds(rows - RIM, RIM)], v_late.at[low], rim_send.at[0], rim_recv.at[0], right)
    to_left = remote(nodes.at[pl.ds(0, RIM)], v_late.at[high], rim_send.at[1], rim_recv.at[1], left)

    @pl.when(has_right)
    def _():
        to_right.start()

    @pl.when(has_left)
    def _():
        to_left.start()

    def push_hub(step, carry):
        hub_copy(step, lambda other: v_hub_src, v_hub, 0).start()
        return carry

    lax.fori_loop(1, blocks, push_hub, 0)

    ready(v_send_id, v_recv_id)
    ids_s, ids_r = v_send_id[...], v_recv_id[...]
    col_s = jnp.transpose(jnp.broadcast_to(ids_s, (LANES, count)))[:, 0:1]
    col_r = jnp.transpose(jnp.broadcast_to(ids_r, (LANES, count)))[:, 0:1]
    own_ids = lax.broadcasted_iota(jnp.int32, (1, rows), 1) + me * rows
    late_count = v_late.shape[0]
    late_row = late_ids(lax.broadcasted_iota(jnp.int32, (1, late_count), 1), me, blocks, rows)
    oh_own[...] = onehot(col_s, own_ids)
    oh_recv[...] = onehot(col_r, own_ids)
    oh_late[...] = onehot(col_s, late_row)

    ready(v_recv, v_send)
    recv_terms = mm(v_nodes[...], v_recv[...]).astype(BF16)
    send_terms = mm(v_nodes[...], v_send[...]).astype(BF16)
    ready(v_edges, v_edge, v_bias)
    v_hidden[...] = (
        mm(v_edges[...], v_edge[...]) + mm(oh_recv[...], recv_terms) + mm(oh_own[...], send_terms) + v_bias[...]
    )

    @pl.when(has_left)
    def _():
        to_right.wait_recv()

    @pl.when(has_right)
    def _():
        to_left.wait_recv()

    hub_wait(v_hub, hub_recv.at[0])
    for r in range(HUB_DEV):
        for j in range(pieces):
            part = v_hub[pl.ds(HUB_DEV * j + r, blocks, stride=tile), :]
            v_late[2 * RIM + r * blocks : 2 * RIM + (r + 1) * blocks, LANES * j : LANES * (j + 1)] = part.astype(BF16)
    late_terms = mm(v_late[...], v_send[...]).astype(BF16)
    v_hidden[...] += mm(oh_late[...], late_terms)

    chunks = [pl.ds(start, CHUNK) for start in range(0, count, CHUNK)]
    for at in chunks:
        pre = v_hidden[at, :]
        sig = sigmoid(pre)
        act = pre * sig
        v_act[at, :] = act.astype(BF16)
        v_slope[at, :] = sig + act * (1.0 - sig)
    ready(v_out, v_gain_e, v_shift_e)
    v_hidden[...] = mm(v_act[...], v_out[...])
    for at in chunks:
        total = v_hidden[at, :]
        centred = total - mean_row(total)
        inv = lax.rsqrt(mean_row(centred * centred) + epsilon)
        normed = centred * inv
        v_normed[at, :] = normed
        v_scale[at, :] = jnp.broadcast_to(inv, (CHUNK, LANES))
        v_new[at, :] = (v_edges[at, :].astype(F32) + normed * v_gain_e[...] + v_shift_e[...]).astype(BF16)

    own_col = lax.broadcasted_iota(jnp.int32, (rows, 1), 0) + me * rows
    t_recv = onehot(own_col, ids_r)
    g_mine[...] = mm(t_recv, v_new[...]).astype(BF16)
    gather_copy = remote(g_mine, g_peer, peer_send.at[0], peer_recv.at[0], peer)
    gather_copy.start()

    ready(v_in, v_bias_n, v_mix, v_gain_n, v_shift_n, v_cot)
    v_pre[...] = mm(v_nodes[...], v_in[0:width, :]) + v_bias_n[...]
    gather_copy.wait_recv()
    gathered = (g_mine[...].astype(F32) + g_peer[...].astype(F32)).astype(BF16)
    pre = v_pre[...] + mm(gathered, v_in[width : 2 * width, :])
    sig = sigmoid(pre)
    act = pre * sig
    v_pre[...] = sig + act * (1.0 - sig)
    mix = mm(act.astype(BF16), v_mix[...])
    centred = mix - mean_row(mix)
    inv = lax.rsqrt(mean_row(centred * centred) + epsilon)
    normed = centred * inv
    o_nodes[...] = (v_nodes[...].astype(F32) + normed * v_gain_n[...] + v_shift_n[...]).astype(BF16)
    store_nodes = pltpu.make_async_copy(o_nodes, out_nodes, store_sem.at[0])
    store_nodes.start()
    scaled = v_cot[...].astype(F32) * v_gain_n[...]
    dmix = (inv * (scaled - mean_row(scaled) - normed * mean_row(scaled * normed))).astype(BF16)
    v_dpre[...] = (mm_t(dmix, v_mix[...]) * v_pre[...]).astype(BF16)
    gathered_grad = mm_t(v_dpre[...], v_in[width : 2 * width, :]).astype(BF16)

    v_up[...] = mm(oh_recv[...], gathered_grad)
    for at in chunks:
        normed = v_normed[at, :]
        scaled = v_up[at, :] * v_gain_e[...]
        v_dsum[at, :] = (
            v_scale[at, 0:1] * (scaled - mean_row(scaled) - normed * mean_row(scaled * normed))
        ).astype(BF16)
    v_hidden[...] = mm_t(v_dsum[...], v_out[...])
    for at in chunks:
        v_edpre[at, :] = (v_hidden[at, :] * v_slope[at, :]).astype(BF16)

    late_col = late_ids(lax.broadcasted_iota(jnp.int32, (late_count, 1), 0), me, blocks, rows)
    t_late = onehot(late_col, ids_s)
    late_sums = mm(t_late, v_edpre[...]).astype(BF16)
    late_part = mm_t(late_sums, v_send[...])
    rim_out[...] = late_part[0 : 2 * RIM, :].astype(BF16)
    back_left = remote(rim_out.at[low], rim_back.at[high], rim_send.at[2], rim_recv.at[2], left)
    back_right = remote(rim_out.at[high], rim_back.at[low], rim_send.at[3], rim_recv.at[3], right)

    @pl.when(has_left)
    def _():
        back_left.start()

    @pl.when(has_right)
    def _():
        back_right.start()

    for r in range(HUB_DEV):
        for j in range(pieces):
            hub_out[pl.ds(HUB_DEV * j + r, blocks, stride=tile), :] = late_part[
                2 * RIM + r * blocks : 2 * RIM + (r + 1) * blocks, LANES * j : LANES * (j + 1)
            ]

    def hub_part(other):
        return hub_out.at[pl.ds(pl.multiple_of(other * tile, tile), tile)]

    def return_hub(step, carry):
        hub_copy(step, hub_part, hub_back, 1).start()
        return carry

    lax.fori_loop(1, blocks, return_hub, 0)

    t_own = onehot(own_col, ids_s)
    t_recv = onehot(own_col, ids_r)
    send_sums = mm(t_own, v_edpre[...]).astype(BF16)
    recv_sums = mm(t_recv, v_edpre[...]).astype(BF16)
    p_mine[...] = (mm_t(send_sums, v_send[...]) + mm_t(recv_sums, v_recv[...])).astype(BF16)
    part_copy = remote(p_mine, p_peer, peer_send.at[1], peer_recv.at[1], peer)
    part_copy.start()

    o_edges[...] = (v_up[...] + mm_t(v_edpre[...], v_edge[...])).astype(BF16)
    store_edges = pltpu.make_async_copy(o_edges, out_edges, store_sem.at[1])
    store_edges.start()
    v_direct[...] = v_cot[...].astype(F32) + mm_t(v_dpre[...], v_in[0:width, :])

    @pl.when(has_right)
    def _():
        back_left.wait_recv()

    @pl.when(has_left)
    def _():
        back_right.wait_recv()

    hub_wait(hub_back, hub_recv.at[1])
    hub_sum = jnp.sum(hub_back[...].reshape(blocks, tile, LANES), axis=0)
    v_up[0:tile, 0:LANES] = hub_sum
    v_hidden[0:16, :] = jnp.zeros((16, width), F32)
    for j in range(pieces):
        v_hidden[0:HUB_DEV, LANES * j : LANES * (j + 1)] = v_up[HUB_DEV * j : HUB_DEV * (j + 1), 0:LANES]
    x_mine[...] = rim_back[...]
    x_mine[0:16, :] = (rim_back[0:16, :].astype(F32) + v_hidden[0:16, :]).astype(BF16)
    last_copy = remote(x_mine, x_peer, peer_send.at[2], peer_recv.at[2], peer)
    last_copy.start()

    part_copy.wait_recv()
    v_direct[...] += p_mine[...].astype(F32) + p_peer[...].astype(F32)
    last_copy.wait_recv()
    extra = x_mine[...].astype(F32) + x_peer[...].astype(F32)
    o_grad[0:RIM, :] = (v_direct[0:RIM, :] + extra[0:RIM]).astype(BF16)
    o_grad[RIM : rows - RIM, :] = v_direct[RIM : rows - RIM, :].astype(BF16)
    o_grad[rows - RIM : rows, :] = (v_direct[rows - RIM : rows, :] + extra[RIM : 2 * RIM]).astype(BF16)
    store_grad = pltpu.make_async_copy(o_grad, out_grad, store_sem.at[2])
    store_grad.start()

    @pl.when(has_right)
    def _():
        to_right.wait_send()
        back_right.wait_send()

    @pl.when(has_left)
    def _():
        to_left.wait_send()
        back_left.wait_send()

    hub_wait(v_hub, hub_send.at[0])
    hub_wait(hub_out, hub_send.at[1])
    gather_copy.wait_send()
    part_copy.wait_send()
    last_copy.wait_send()
    store_nodes.wait()
    store_edges.wait()
    store_grad.wait()


def body(
    nodes, edges, senders, receivers, edge_proj, send_proj, recv_proj, edge_bias, edge_out, edge_gain, edge_shift,
    node_in, node_bias, node_out, node_gain, node_shift, node_cot,
):
    blocks = lax.axis_size("space")
    rows, width = nodes.shape
    count = edges.shape[0]
    tile = HUB_DEV * (width // LANES)
    late = 2 * RIM + HUB_DEV * blocks

    def line(vec):
        return vec.reshape(1, -1)

    args = (
        line(senders), line(receivers), nodes, edges, edge_proj, send_proj, recv_proj, line(edge_bias), edge_out,
        line(edge_gain), line(edge_shift), node_in, line(node_bias), node_out, line(node_gain), line(node_shift), node_cot,
    )
    any_spec = pl.BlockSpec(memory_space=pl.ANY)
    vmem = pltpu.VMEM
    dma = pltpu.SemaphoreType.DMA
    scratch = [vmem(a.shape, a.dtype) for a in args] + [
        vmem((late, width), BF16),
        vmem((tile, LANES), F32),
        vmem((blocks * tile, LANES), F32),
        vmem((count, rows), BF16),
        vmem((count, rows), BF16),
        vmem((count, late), BF16),
        vmem((count, width), F32),
        vmem((count, width), F32),
        vmem((count, width), BF16),
        vmem((count, width), F32),
        vmem((count, LANES), F32),
        vmem((count, width), BF16),
        vmem((rows, width), BF16),
        vmem((rows, width), BF16),
        vmem((rows, width), F32),
        vmem((rows, width), BF16),
        vmem((rows, width), F32),
        vmem((count, width), F32),
        vmem((count, width), BF16),
        vmem((count, width), BF16),
        vmem((2 * RIM, width), BF16),
        vmem((2 * RIM, width), BF16),
        vmem((blocks * tile, LANES), F32),
        vmem((blocks * tile, LANES), F32),
        vmem((rows, width), BF16),
        vmem((rows, width), BF16),
        vmem((2 * RIM, width), BF16),
        vmem((2 * RIM, width), BF16),
        vmem((rows, width), BF16),
        vmem((rows, width), BF16),
        vmem((count, width), BF16),
        dma((len(args),)),
        dma((3,)),
        dma((4,)),
        dma((4,)),
        dma((2,)),
        dma((2,)),
        dma((3,)),
        dma((3,)),
    ]
    return pl.pallas_call(
        functools.partial(kernel, blocks),
        out_shape=(
            jax.ShapeDtypeStruct((rows, width), BF16),
            jax.ShapeDtypeStruct((rows, width), BF16),
            jax.ShapeDtypeStruct((count, width), BF16),
        ),
        in_specs=[any_spec] * len(args),
        out_specs=(any_spec,) * 3,
        scratch_shapes=scratch,
        compiler_params=pltpu.CompilerParams(
            collective_id=0, has_side_effects=True, vmem_limit_bytes=60 * 1024 * 1024
        ),
    )(*args)


def solution(mesh):
    in_specs = (
        P("space", None),
        P(("space", "feat"), None),
        P(("space", "feat")),
        P(("space", "feat")),
        *([P()] * 12),
        P("space", None),
    )
    out_specs = (P("space", None), P("space", None), P(("space", "feat"), None))
    return jax.shard_map(body, mesh=mesh, in_specs=in_specs, out_specs=out_specs, check_vma=False)
```

time: 217 us -> 29.5 us (0.14)
  blocking collectives: 123 us -> 0 us
  waiting for transfers between devices: 35.8 us -> 0 us
  Pallas kernels: 0 us -> 22.7 us
  matrix products: 19.2 us -> 0 us
  between operations: 15.2 us -> 0.66 us
  starting transfers between devices: 9.55 us -> 0 us
  other arithmetic: 5.47 us -> 0 us
    unnamed x1 -> x0, blocking collectives: 77.6 us -> none
    all_gather x4 -> x0, blocking collectives: 45.6 us -> none  [the longest x1 39.5 us: body(): coarse = lax.all_gather(carried[:HUB_DEV], 'space', axis=0, tiled=True)]
    psum x2 -> x0, waiting for transfers between devices: 32 us -> none  [feat_total(): return lax.psum(partial_sum, 'feat')]
    pallas_call x0 -> x1, Pallas kernels: none -> 22.7 us  [body(): pl.pallas_call(functools.partial(kernel, blocks), out_shape=(jax.ShapeDty...]
    dot_general x18 -> x0, matrix products: 19.2 us -> none  [the longest x3 4.05 us: exact_dot(): return jnp.dot(left, right, precision=lax.Precision.HIGHEST)]
    ppermute x4 -> x0, starting transfers between devices: 9.47 us -> none  [the longest x2 6.88 us: padded(): lax.ppermute(lax.slice_in_dim(block, block.shape[dim] - width, None, axis...]
    ppermute x4 -> x0, waiting for transfers between devices: 3.72 us -> none  [the longest x2 3.71 us: padded(): lax.ppermute(lax.slice_in_dim(block, 0, width, axis=dim), axis, backward)]
    reduce_sum x4 -> x0, other arithmetic: 3.07 us -> none  [the longest x1 1.7 us: layer_stats(): average = jnp.mean(values, axis=-1, keepdims=True)]
  transfers between devices with their start and end apart: 6 -> 0, of which waited for: 3 -> 0; matrix products, arithmetic and copies ran while one was open for 2% -> 0% of each run, Pallas kernels for 0% -> 0%
where the time goes in v1:
time: 29.5 us; the launch traced here: 29.3 us
  Pallas kernels  22.7 us (77%)
  local copies, waits for them, and re-layouts  5.9 us (20%)
  between operations  0.66 us (2%)
    pallas_call x1, Pallas kernels, body(): pl.pallas_call(functools.partial(kernel, blocks), out_shape=(jax.ShapeDty...  22.7 us
    unnamed x9, local copies, waits for them, and re-layouts  4.78 us
    reshape x2, local copies, waits for them, and re-layouts, line(): return vec.reshape(1, -1)  1.13 us

profile of v1, /device:TPU:0, one launch (start us, length us, event | category | flops | bytes accessed | tf_op | source)
XLA Modules:
  0.0 29.3 jit_solution(387670528760556553)
XLA Ops:
  0.6 0.0 copy-start.1
  0.6 0.7 %copy-done.1 = s32[384]{0:T(512)S(1)} copy-done((s32[384]{0:T(512)S(1)}, s32[384]{0:T(512)}, u32[]{:S(2)}) %copy-start.1) | copy-done | bytes 1560
  1.3 0.0 copy-start.2
  1.3 0.6 %reshape.30.send_id = s32[1,384]{1,0:T(1,128)} reshape(s32[384]{0:T(512)S(1)} %copy-done.1) | data formatting | bytes 3072 | tf_op jit(solution)/shard_map/reshape | solution.py:349
  1.9 0.1 copy-done.2
  2.0 0.6 %reshape.31.recv_id = s32[1,384]{1,0:T(1,128)} reshape(s32[384]{0:T(512)S(1)} %copy-done.2) | data formatting | bytes 3072 | tf_op jit(solution)/shard_map/reshape | solution.py:349
  2.6 22.7 %shard_map.184 = (bf16[160,512]{1,0:T(8,128)(2,1)}, bf16[160,512]{1,0:T(8,128)(2,1)}, bf16[384,512]{1,0:T(8,128)(2,1)}) custom-call(s32[1,384]{1,0:T(1,128)} %reshape.30.send_id, s32[1,384]{1,0:T(1,128)} %reshape.31.recv_id, bf16[160,512]{1,0:T(8,128)(2,1)} %nodes.1, bf16[384,512]{1,0:T(8,128)(2,1)} %edges.1, bf16[512,512]{1,0:T(8,128)(2,1)} %w_edge.1, ...), custom_call_target="tpu_custom_call" | custom-call | tf_op jit(solution)/shard_map/pallas_call | solution.py:399
  25.3 0.0 copy-start
  25.3 1.6 %copy.23 = bf16[160,512]{1,0:T(8,128)(2,1)} copy(bf16[160,512]{1,0:T(8,128)(2,1)} %get-tuple-element.6) | data formatting | bytes 327680
  26.9 1.6 %copy.24 = bf16[160,512]{1,0:T(8,128)(2,1)} copy(bf16[160,512]{1,0:T(8,128)(2,1)} %get-tuple-element.7) | data formatting | bytes 327680
  28.5 0.0 copy-done
  28.5 0.7 %copy.25 = bf16[384,512]{1,0:T(8,128)(2,1)} copy(bf16[384,512]{1,0:T(8,128)(2,1)S(1)} %copy-done) | data formatting | bytes 786432
Async XLA Ops:
  0.6 0.7 %copy-start.1 = (s32[384]{0:T(512)S(1)}, s32[384]{0:T(512)}, u32[]{:S(2)}) copy-start(s32[384]{0:T(512)} %param.19) | copy-start | bytes 4612
  1.3 0.7 %copy-start.2 = (s32[384]{0:T(512)S(1)}, s32[384]{0:T(512)}, u32[]{:S(2)}) copy-start(s32[384]{0:T(512)} %param.20) | copy-start | bytes 4612
  25.3 3.2 %copy-start = (bf16[384,512]{1,0:T(8,128)(2,1)S(1)}, bf16[384,512]{1,0:T(8,128)(2,1)}, u32[]{:S(2)}) copy-start(bf16[384,512]{1,0:T(8,128)(2,1)} %get-tuple-element.8) | copy-start | bytes 1179652
